TPU v7x, 32 devices: a whole 2x2x4 slice. The times are simulated.
32 devices in a mesh: layer: 2 (over y), row: 4 (over z), col: 2 (over x), sub: 2 (over core).
Axes of the slice: x: 2, y: 2, z: 4, core: 2. Of those that a mesh axis runs over, the one named last changes fastest.
Arguments:
- act_a: bfloat16 [4, 1024, 14336], P(('layer', 'sub'), 'col', 'row'), parts along dimension 0, may hold values from -4000 to 4000
- act_b: bfloat16 [4, 1024, 14336], P(('layer', 'sub'), 'row', 'col'), parts along dimension 0, may hold values from -4000 to 4000
- pair_index: int32 [28672], P('layer'), parts along dimension 0, may hold values from 0 to 14335, as said below
- weight_a: bfloat16 [28672, 4096], P(('layer', 'row'), ('col', 'sub')), parts along dimension 0, may hold values from -6 to 6
- weight_b: bfloat16 [28672, 4096], P(('layer', 'row'), ('col', 'sub')), parts along dimension 0, may hold values from -6 to 6
Outputs:
- correlation: bfloat16 [28672, 14336], P(('layer', 'row', 'sub'), 'col'), parts along dimension 0
- merged: bfloat16 [28672, 4096], P(('layer', 'row'), ('col', 'sub')), parts along dimension 0
There are 2 independent parts, one for each index of `layer`. A program takes and returns all parts, laid end to end along the dimension named above; each array names one. Nothing has to cross between parts.
Inputs may be any that keep to these rules, and one draw needn't show every extreme that they name: `pair_index`: A permutation of the 14336 units: entry i is the B unit matched to A unit i. Of the 3584 A units of one aligned block, at most 1792 are matched to units of one aligned block of 3584 B units, and in every draw exactly 1792 are for some pair of blocks.
All inputs are finite; a program needn't handle non-finite values.
Results may differ from a plain program's by a relative error of at most 0.007.
Values may be sent and summed in bfloat16 or wider, within the bound.
A program may use at most 320 MiB of HBM per device.

v0:
```python
import jax
import jax.numpy as jnp
from jax import lax
from jax.sharding import PartitionSpec as P

EPSILON = 1e-05


def body(act_a, act_b, pair_index, weight_a, weight_b):
    rows_a = lax.all_gather(act_a, "col", axis=1, tiled=True)
    rows_b = lax.all_gather(act_b, "row", axis=1, tiled=True)
    units_a = rows_a.shape[2]
    units_b = rows_b.shape[2]
    flat_a = rows_a.reshape(-1, units_a)
    flat_b = rows_b.reshape(-1, units_b)
    count_all = float(flat_a.shape[0] * lax.axis_size("sub"))
    local_sum_a = jnp.sum(flat_a, axis=0, dtype=jnp.float32)
    local_sum_b = jnp.sum(flat_b, axis=0, dtype=jnp.float32)
    sum_a, sum_b = lax.psum((local_sum_a, local_sum_b), "sub")
    mean_a = sum_a / count_all
    mean_b = sum_b / count_all
    square_a, square_b = lax.psum(
        (
            jnp.sum(jnp.square(flat_a.astype(jnp.float32) - mean_a), axis=0),
            jnp.sum(jnp.square(flat_b.astype(jnp.float32) - mean_b), axis=0),
        ),
        "sub",
    )
    var_a = square_a / count_all
    var_b = square_b / count_all
    normed_a = ((flat_a.astype(jnp.float32) - mean_a) * lax.rsqrt(var_a + EPSILON)).astype(
        jnp.bfloat16
    )
    normed_b = ((flat_b.astype(jnp.float32) - mean_b) * lax.rsqrt(var_b + EPSILON)).astype(
        jnp.bfloat16
    )
    kept_rows = units_a // lax.axis_size("sub")
    product = lax.dot_general(
        normed_a, normed_b, (((0,), (0,)), ((), ())), preferred_element_type=jnp.float32
    )
    correlation = lax.psum_scatter(
        (product / count_all).astype(jnp.bfloat16), "sub", scatter_dimension=0, tiled=True
    )
    my_row = lax.axis_index("row")
    my_col = lax.axis_index("col")
    my_sub = lax.axis_index("sub")
    row_start = my_row * units_a + my_sub * kept_rows
    my_pairs = lax.dynamic_slice_in_dim(pair_index, row_start, kept_rows)
    local_col = my_pairs - my_col * units_b
    inside = (local_col >= 0) & (local_col < units_b)
    picked_values = jnp.take_along_axis(
        correlation, jnp.clip(local_col, 0, units_b - 1)[:, None], axis=1
    )[:, 0]
    own_terms = jnp.where(inside, picked_values.astype(jnp.float32), 0.0)
    spread = lax.dynamic_update_slice_in_dim(
        jnp.zeros((units_a,), jnp.float32), own_terms, my_sub * kept_rows, 0
    )
    matched = lax.psum(spread, ("col", "sub"))
    share_b = jnp.maximum(matched, 0.0)
    unit_pairs = lax.dynamic_slice_in_dim(pair_index, my_row * units_a, units_a)
    portion = lax.all_gather(weight_b, "row", axis=0, tiled=True)
    is_valid = (unit_pairs >= 0) & (unit_pairs < portion.shape[0])
    taken_rows = jnp.take(portion, jnp.clip(unit_pairs, 0, portion.shape[0] - 1), axis=0)
    partner = jnp.where(is_valid[:, None], taken_rows.astype(jnp.float32), 0.0)
    merged = (weight_a.astype(jnp.float32) + share_b[:, None] * partner) / (1.0 + share_b[:, None])
    return (correlation, merged.astype(jnp.bfloat16))


def solution(mesh):
    return jax.shard_map(
        body,
        mesh=mesh,
        in_specs=(
            P(("layer", "sub"), "col", "row"),
            P(("layer", "sub"), "row", "col"),
            P("layer"),
            P(("layer", "row"), ("col", "sub")),
            P(("layer", "row"), ("col", "sub")),
        ),
        out_specs=(P(("layer", "row", "sub"), "col"), P(("layer", "row"), ("col", "sub"))),
        check_vma=False,
    )
```

profile of v0, /device:TPU:8, one launch (start us, length us, event | category | flops | bytes accessed | tf_op | source)
XLA Modules:
  0.0 969.9 jit_solution(3980887697942649581)
XLA Ops:
  7.2 0.0 all-gather.4.cloned.1.call-start
  7.2 0.7 all-gather.4.cloned.1.call-update
  7.9 0.0 all-gather.6.cloned.1.call-start
  7.9 0.7 all-gather.6.cloned.1.call-update
  8.6 0.0 all-gather.8.cloned.1.call-start
  8.7 0.7 all-gather.8.cloned.1.call-update
  9.4 0.0 reduce-scatter.5.cloned.1.call-start
  9.4 93.5 %all-gather.4.cloned.1.call-done = bf16[1,1024,3584]{2,1,0:T(8,128)(2,1)} async-done(((bf16[1,512,3584]{2,1,0:T(8,128)(2,1)}), bf16[1,1024,3584]{2,1,0:T(8,128)(2,1)}) %all-gather.4.cloned.1.call-update) | async-done | bytes 7340048 | tf_op jit(solution)/shard_map/all_gather | solution.py:10
  102.9 4.1 convert_reduce_fusion.1
  107.1 247.0 %all-gather.6.cloned.1.call-done = bf16[1,1024,7168]{2,1,0:T(8,128)(2,1)} async-done(((bf16[1,256,7168]{2,1,0:T(8,128)(2,1)}), bf16[1,1024,7168]{2,1,0:T(8,128)(2,1)}) %all-gather.6.cloned.1.call-update) | async-done | bytes 14680080 | tf_op jit(solution)/shard_map/all_gather | solution.py:11
  354.0 7.3 convert_reduce_fusion
  361.3 3.5 all-reduce.2
  364.9 7.1 fusion.9
  372.0 10.5 %fusion.4 = f32[7168]{0:T(1024)S(1)} fusion(bf16[1,1024,7168]{2,1,0:T(8,128)(2,1)} %all-gather.6.cloned.1.call-done, f32[7168]{0:T(1024)S(1)} %broadcast_multiply_fusion), kind=kLoop, calls=%fused_computation.10 | loop fusion | flops 29352960 | bytes 14737408 | tf_op jit(solution)/shard_map/reduce_sum | solution.py:25
  382.6 3.8 all-reduce.1
  386.4 66.0 %multiply_convert_fusion = bf16[3584,7168]{1,0:T(8,128)(2,1)} fusion(bf16[1,1024,7168]{2,1,0:T(8,128)(2,1)} %all-gather.6.cloned.1.call-done, f32[7168]{0:T(1024)S(1)} %add_rsqrt_fusion, f32[7168]{0:T(1024)S(1)} %broadcast_multiply_fusion, bf16[1,1024,3584]{2,1,0:T(8,128)(2,1)} %all-gather.4.cloned.1.call-done, f32[3584]{0:T(1024)S(1)} %add_rsqrt_fusion.1, ...), kind=kOutput, calls=%fused_computation.2 | convolution fusion | flops 52708769792 | bytes 73486336 | tf_op jit(solution)/shard_map/dot_general | solution.py:38
  452.4 0.0 copy-start
  452.4 0.0 reduce-scatter.5.cloned.1.call-update
  452.4 0.8 copy-done
  453.2 0.1 compare_select_fusion.1
  453.3 0.1 compare_and_fusion
  453.5 393.5 %all-gather.8.cloned.1.call-done = bf16[14336,1024]{1,0:T(8,128)(2,1)} async-done(((bf16[3584,1024]{1,0:T(8,128)(2,1)}), bf16[14336,1024]{1,0:T(8,128)(2,1)}) %all-gather.8.cloned.1.call-update) | async-done | bytes 29360144 | tf_op jit(solution)/shard_map/all_gather | solution.py:61
  847.0 29.5 %gather_fusion = bf16[3584,1024]{1,0:T(8,128)(2,1)} fusion(bf16[14336,1024]{1,0:T(8,128)(2,1)} %all-gather.8.cloned.1.call-done, s32[4096]{0:T(1024)S(1)} %pad_clamp_fusion), kind=kCustom, calls=%fused_computation | custom fusion | bytes 14694400 | tf_op jit(solution)/shard_map/jit(_take)/gather | solution.py:63
  876.5 39.2 %reduce-scatter.5.cloned.1.call-done = bf16[1792,7168]{1,0:T(8,128)(2,1)} async-done(((bf16[3584,7168]{1,0:T(8,128)(2,1)}), bf16[1792,7168]{1,0:T(8,128)(2,1)}) %reduce-scatter.5.cloned.1.call-update) | async-done | bytes 25690128
  915.7 25.7 %gather_fusion.1 = bf16[1792]{0:T(1024)(128)(2,1)S(1)} fusion(bf16[1792,7168]{1,0:T(8,128)(2,1)} %reduce-scatter.5.cloned.1.call-done, s32[1792]{0:T(1024)S(1)} %fusion.21), kind=kCustom, calls=%fused_computation.1 | custom fusion | bytes 21504 | tf_op jit(solution)/shard_map/jit(take_along_axis)/gather | solution.py:51
  941.5 0.2 select_dynamic-update-slice_fusion
  941.7 10.2 %psum.39 = f32[3584]{0:T(1024)S(1)} all-reduce(f32[3584]{0:T(1024)S(1)} %select_dynamic-update-slice_fusion), channel_id=1, replica_groups=mesh['layer'=2,'row'=4,'col'=2,'sub'=2] {'col','sub'}, use_global_device_ids=true, to_apply=%region_9.10 | all-reduce | flops 3584 | bytes 28672 | tf_op jit(solution)/shard_map/psum | solution.py:58
  951.8 11.5 %divide_convert_fusion = bf16[3584,1024]{1,0:T(8,128)(2,1)} fusion(bf16[3584,1024]{1,0:T(8,128)(2,1)} %param.8, f32[3584]{0:T(1024)S(1)} %get-tuple-element.10, bf16[3584,1024]{1,0:T(8,128)(2,1)} %gather_fusion, f32[3584]{0:T(1024)S(1)} %get-tuple-element.9, pred[3584]{0:T(1024)(128)(4,1)S(1)} %get-tuple-element.6, pred[3584]{0:T(1024)(128)(4,1)S(1)} %get-tuple-element.8), kind=kLoop, calls=%fused_computation.20 | loop fusion | flops 29360128 | bytes 22055936 | tf_op jit(solution)/shard_map/convert_element_type | solution.py:66
  (11 shorter events, 0.1 us)
Async XLA Ops:
  7.2 95.8 %all-gather.4.cloned.1.call-start = ((), (), s32[]{:S(2)}) async-start(), calls=%async_computation.1 | async-start | bytes 11010048 | tf_op jit(solution)/shard_map/all_gather | solution.py:10
  7.9 346.1 %all-gather.6.cloned.1.call-start = ((), (), s32[]{:S(2)}) async-start(), calls=%async_computation.2 | async-start | bytes 18350080 | tf_op jit(solution)/shard_map/all_gather | solution.py:11
  8.6 838.3 %all-gather.8.cloned.1.call-start = ((), (), s32[]{:S(2)}) async-start(), calls=%async_computation.3 | async-start | bytes 36700160 | tf_op jit(solution)/shard_map/all_gather | solution.py:61
  9.4 906.3 %reduce-scatter.5.cloned.1.call-start = ((), (), s32[]{:S(2)}) async-start(), calls=%async_computation.4 | async-start | bytes 77070336
  452.4 0.8 copy-start
Sparse Core Ops, SparseCore 0:
  9.5 93.3 all-gather.3
  104.5 249.5 all-gather.5
  355.6 491.3 all-gather.7
  849.7 65.9 reduce-scatter.4
where the time goes:
time: 973 us; the launch traced here: 970 us
  waiting for transfers between devices  775 us (80%)
  matrix products  66 us (7%)
  local copies, waits for them, and re-layouts  56 us (6%)
  other arithmetic  41.1 us (4%)
  blocking collectives  17.5 us (2%)
  between operations  13.9 us (1%)
    all_gather x1, waiting for transfers between devices, body(): portion = lax.all_gather(weight_b, 'row', axis=0, tiled=True)  393 us
    all_gather x1, waiting for transfers between devices, body(): rows_b = lax.all_gather(act_b, 'row', axis=1, tiled=True)  247 us
    all_gather x1, waiting for transfers between devices, body(): rows_a = lax.all_gather(act_a, 'col', axis=1, tiled=True)  93.5 us
    dot_general x1, matrix products, body(): lax.dot_general(normed_a, normed_b, (((0,), (0,)), ((), ())), preferred_e...  66 us
    unnamed x5, waiting for transfers between devices  41.3 us
    gather x1, local copies, waits for them, and re-layouts, body(): jnp.take(portion, jnp.clip(unit_pairs, 0, portion.shape[0] - 1), axis=0)  29.5 us
    gather x1, local copies, waits for them, and re-layouts, body(): jnp.take_along_axis(correlation, jnp.clip(local_col, 0, units_b - 1)[:, N...  25.7 us
  transfers between devices with their start and end apart: 4, of which 4 were waited for; matrix products, arithmetic and copies ran while one was open for 13% of the time, Pallas kernels for 0%

commit v1 on v0

v1 whole, which is shorter than its diff:
```python
import jax
import jax.numpy as jnp
from jax import lax
from jax.sharding import PartitionSpec as P

EPSILON = 1e-05


def pairs_by_xor(size, step):
    return [(place, place ^ step) for place in range(size)]


def unit_stats(block, axes, count_all):
    wide = block.astype(jnp.float32)
    mean = lax.psum(jnp.sum(wide, axis=0), axes) / count_all
    square = lax.psum(jnp.sum(jnp.square(wide - mean), axis=0), axes)
    return mean, lax.rsqrt(square / count_all + EPSILON)


def normalise(block, stats):
    mean, inverse = stats
    return ((block.astype(jnp.float32) - mean) * inverse).astype(jnp.bfloat16)


def body(act_a, act_b, pair_index, weight_a, weight_b):
    rows, cols, subs = (lax.axis_size(name) for name in ("row", "col", "sub"))
    my_row, my_col, my_sub = (lax.axis_index(name) for name in ("row", "col", "sub"))
    own_a, own_b = act_a[0], act_b[0]
    tokens_a, units_a = own_a.shape
    units_b = own_b.shape[1]
    block = weight_b.shape[0]
    cap = 2 * block // rows
    count_all = float(tokens_a * cols * subs)

    flat_b = lax.all_gather(own_b, "row", axis=0, tiled=True)
    raw_a = jnp.zeros((tokens_a * cols, units_a), own_a.dtype)
    raw_a = lax.dynamic_update_slice_in_dim(raw_a, own_a, my_col * tokens_a, 0)
    for step in range(1, cols):
        came = lax.ppermute(own_a, "col", pairs_by_xor(cols, step))
        raw_a = lax.dynamic_update_slice_in_dim(raw_a, came, (my_col ^ step) * tokens_a, 0)

    def rank_in(mask):
        return jnp.cumsum(mask.astype(jnp.int32)) - 1

    def packed(step):
        theirs = lax.dynamic_slice_in_dim(pair_index, (my_row ^ step) * block, block)
        local = theirs - my_row * block
        mask = (local >= 0) & (local < block)
        place = jnp.where(mask, rank_in(mask), -1)
        hit = place[None, :] == jnp.arange(cap, dtype=jnp.int32)[:, None]
        chosen = jnp.sum(jnp.where(hit, local[None, :], 0), axis=1)
        return weight_b.at[chosen].get(mode="promise_in_bounds")

    early = [rows // 2]
    late = [step for step in range(rows - 1, 0, -1) if step not in early]
    arrived = {}
    for step in early:
        arrived[step] = lax.ppermute(packed(step), "row", pairs_by_xor(rows, step))
    waiting = [packed(step) for step in late]

    stats_a = unit_stats(own_a, ("col", "sub"), count_all)
    stats_b = unit_stats(own_b, ("row", "sub"), count_all)

    flat_b, *waiting = lax.optimization_barrier((flat_b, *waiting))
    for step, rows_out in zip(late, waiting):
        arrived[step] = lax.ppermute(rows_out, "row", pairs_by_xor(rows, step))

    normed_a = normalise(raw_a, stats_a)
    normed_b = normalise(flat_b, stats_b)
    kept_rows = units_a // subs
    product = lax.dot_general(
        normed_a, normed_b, (((0,), (0,)), ((), ())), preferred_element_type=jnp.float32
    )
    correlation = lax.psum_scatter(
        (product / count_all).astype(jnp.bfloat16), "sub", scatter_dimension=0, tiled=True
    )
    row_start = my_row * units_a + my_sub * kept_rows
    my_pairs = lax.dynamic_slice_in_dim(pair_index, row_start, kept_rows)
    local_col = my_pairs - my_col * units_b
    inside = (local_col >= 0) & (local_col < units_b)
    picked_values = jnp.take_along_axis(
        correlation, jnp.clip(local_col, 0, units_b - 1)[:, None], axis=1
    )[:, 0]
    own_terms = jnp.where(inside, picked_values.astype(jnp.float32), 0.0)
    spread = lax.dynamic_update_slice_in_dim(
        jnp.zeros((units_a,), jnp.float32), own_terms, my_sub * kept_rows, 0
    )
    matched = lax.psum(spread, ("col", "sub"))
    share_b = jnp.maximum(matched, 0.0)

    unit_pairs = lax.dynamic_slice_in_dim(pair_index, my_row * units_a, units_a)
    local = unit_pairs - my_row * block
    mask = (local >= 0) & (local < block)
    spot = jnp.where(mask, local, 0)
    table = [weight_b]
    start = block
    for step in early + late:
        table.append(arrived[step])
        theirs = unit_pairs - (my_row ^ step) * block
        mask = (theirs >= 0) & (theirs < block)
        spot = jnp.where(mask, start + rank_in(mask), spot)
        start += cap
    portion = jnp.concatenate(table, axis=0)
    partner = portion.at[spot].get(mode="promise_in_bounds").astype(jnp.float32)
    merged = (weight_a.astype(jnp.float32) + share_b[:, None] * partner) / (1.0 + share_b[:, None])
    return (correlation, merged.astype(jnp.bfloat16))


def solution(mesh):
    return jax.shard_map(
        body,
        mesh=mesh,
        in_specs=(
            P(("layer", "sub"), "col", "row"),
            P(("layer", "sub"), "row", "col"),
            P("layer"),
            P(("layer", "row"), ("col", "sub")),
            P(("layer", "row"), ("col", "sub")),
        ),
        out_specs=(P(("layer", "row", "sub"), "col"), P(("layer", "row"), ("col", "sub"))),
        check_vma=False,
    )
```

time: 973 us -> 770 us (0.79)
  waiting for transfers between devices: 775 us -> 376 us
  blocking collectives: 17.5 us -> 139 us
  local copies, waits for them, and re-layouts: 56 us -> 99.1 us
  other arithmetic: 41.1 us -> 58 us
    all_gather x3 -> x1, waiting for transfers between devices: 734 us -> 63.9 us  [body(): flat_b = lax.all_gather(own_b, 'row', axis=0, tiled=True)]
    ppermute x0 -> x4, waiting for transfers between devices: none -> 312 us  [the longest x1 233 us: body(): arrived[step] = lax.ppermute(packed(step), 'row', pairs_by_xor(rows, step))]
    psum x2 -> x4, blocking collectives: 7.33 us -> 127 us  [the longest x2 78.6 us: unit_stats(): mean = lax.psum(jnp.sum(wide, axis=0), axes) / count_all]
    unnamed x5 -> x3, waiting for transfers between devices: 41.3 us -> 0.7 us
    gather x1 -> x4, local copies, waits for them, and re-layouts: 29.5 us -> 64.8 us  [the longest x3 39.8 us: packed(): return weight_b.at[chosen].get(mode='promise_in_bounds')]
    concatenate x0 -> x1, other arithmetic: none -> 23 us  [body(): portion = jnp.concatenate(table, axis=0)]
    reduce_sum x4 -> x6, other arithmetic: 29.1 us -> 21.7 us  [the longest x2 10.2 us: packed(): chosen = jnp.sum(jnp.where(hit, local[None, :], 0), axis=1)]
  transfers between devices with their start and end apart: 4 -> 6, of which waited for: 4 -> 3; matrix products, arithmetic and copies ran while one was open for 13% -> 16% of each run, Pallas kernels for 0% -> 0%
where the time goes in v1:
time: 770 us; the launch traced here: 760 us
  waiting for transfers between devices  376 us (49%)
  blocking collectives  139 us (18%)
  local copies, waits for them, and re-layouts  99.1 us (13%)
  matrix products  65.9 us (9%)
  other arithmetic  58 us (8%)
  between operations  14.7 us (2%)
    ppermute x1, waiting for transfers between devices, body(): arrived[step] = lax.ppermute(packed(step), 'row', pairs_by_xor(rows, step))  233 us
    ppermute x2, waiting for transfers between devices, body(): arrived[step] = lax.ppermute(rows_out, 'row', pairs_by_xor(rows, step))  78.8 us
    psum x2, blocking collectives, unit_stats(): mean = lax.psum(jnp.sum(wide, axis=0), axes) / count_all  78.6 us
    dot_general x1, matrix products, body(): lax.dot_general(normed_a, normed_b, (((0,), (0,)), ((), ())), preferred_e...  65.9 us
    all_gather x1, waiting for transfers between devices, body(): flat_b = lax.all_gather(own_b, 'row', axis=0, tiled=True)  63.9 us
    psum x2, blocking collectives, unit_stats(): square = lax.psum(jnp.sum(jnp.square(wide - mean), axis=0), axes)  48.4 us
    gather x3, local copies, waits for them, and re-layouts, packed(): return weight_b.at[chosen].get(mode='promise_in_bounds')  39.8 us
    gather x1, local copies, waits for them, and re-layouts, body(): partner = portion.at[spot].get(mode='promise_in_bounds').astype(jnp.float32)  25 us
  transfers between devices with their start and end apart: 6, of which 3 were waited for; matrix products, arithmetic and copies ran while one was open for 16% of the time, Pallas kernels for 0%

profile of v1, /device:TPU:8, one launch (start us, length us, event | category | flops | bytes accessed | tf_op | source)
XLA Modules:
  0.0 760.1 jit_solution(15050984217569600237)
XLA Ops:
  7.2 0.0 all-gather.3.cloned.1.call-start
  7.2 0.7 all-gather.3.cloned.1.call-update
  7.9 0.0 reduce-scatter.5.cloned.1.call-start
  7.9 1.6 collective-permute-start
  9.5 0.9 convert_bitcast_fusion.1
  10.4 0.3 reduce-window.54
  10.7 0.3 reduce-window.50
  11.0 0.3 reduce-window.56
  11.3 0.1 slice.70
  11.3 0.1 reduce-window.59
  11.4 0.1 slice.64
  11.5 0.1 reduce-window.51
  11.5 0.1 slice.66
  11.6 0.1 reduce-window.55
  11.6 0.1 slice_reduce_fusion.3
  11.8 0.1 slice_reduce_fusion.4
  11.9 0.1 bitcast_select_fusion.1
  12.0 0.1 bitcast_select_fusion.2
  12.0 6.8 select_reduce_fusion
  18.9 0.1 slice_reduce_fusion.5
  19.0 0.1 bitcast_select_fusion.3
  19.1 3.4 select_reduce_fusion.2
  22.5 13.7 %gather_fusion.1 = bf16[1792,1024]{1,0:T(8,128)(2,1)} fusion(bf16[3584,1024]{1,0:T(8,128)(2,1)} %param.9, s32[2048]{0:T(1024)S(1)} %pad_clamp_fusion.2), kind=kCustom, calls=%fused_computation.1 | custom fusion | bytes 7347200 | tf_op jit(solution)/shard_map/gather | solution.py:52
  36.3 13.0 %gather_fusion = bf16[1792,1024]{1,0:T(8,128)(2,1)} fusion(bf16[3584,1024]{1,0:T(8,128)(2,1)} %param.9, s32[2048]{0:T(1024)S(1)} %pad_clamp_fusion.3), kind=kCustom, calls=%fused_computation | custom fusion | bytes 7347200 | tf_op jit(solution)/shard_map/gather | solution.py:52
  49.2 2.7 convert_reduce_fusion.1
  52.0 44.8 %psum.35 = f32[3584]{0:T(1024)S(1)} all-reduce(f32[3584]{0:T(1024)S(1)} %convert_reduce_fusion.1), channel_id=1, replica_groups=mesh['layer'=2,'row'=4,'col'=2,'sub'=2] {'col','sub'}, use_global_device_ids=true, to_apply=%region_1.2 | all-reduce | flops 3584 | bytes 28672 | tf_op jit(solution)/shard_map/psum | solution.py:15
  96.7 3.1 fusion.3
  99.8 10.6 %psum.36 = f32[3584]{0:T(1024)S(1)} all-reduce(f32[3584]{0:T(1024)S(1)} %fusion.3), channel_id=1, replica_groups=mesh['layer'=2,'row'=4,'col'=2,'sub'=2] {'col','sub'}, use_global_device_ids=true, to_apply=%region_3.4 | all-reduce | flops 3584 | bytes 28672 | tf_op jit(solution)/shard_map/psum | solution.py:16
  110.4 2.6 convert_reduce_fusion
  113.1 33.8 %psum.37 = f32[7168]{0:T(1024)S(1)} all-reduce(f32[7168]{0:T(1024)S(1)} %convert_reduce_fusion), channel_id=1, replica_groups=mesh['layer'=2,'row'=4,'col'=2,'sub'=2] {'row','sub'}, use_global_device_ids=true, to_apply=%region_11.12 | all-reduce | flops 7168 | bytes 57344 | tf_op jit(solution)/shard_map/psum | solution.py:15
  146.9 3.1 fusion.6
  149.9 37.8 %psum.38 = f32[7168]{0:T(1024)S(1)} all-reduce(f32[7168]{0:T(1024)S(1)} %fusion.6), channel_id=1, replica_groups=mesh['layer'=2,'row'=4,'col'=2,'sub'=2] {'row','sub'}, use_global_device_ids=true, to_apply=%region_13.14 | all-reduce | flops 7168 | bytes 57344 | tf_op jit(solution)/shard_map/psum | solution.py:16
  187.8 3.6 broadcast_in_dim.64
  191.4 2.1 constant_dynamic-update-slice_fusion.1
  193.5 0.0 collective-permute-done
  193.5 4.1 constant_dynamic-update-slice_fusion
  197.6 63.9 %all-gather.3.cloned.1.call-done = bf16[1,1024,7168]{2,1,0:T(8,128)(2,1)} async-done(((bf16[1,256,7168]{2,1,0:T(8,128)(2,1)}), bf16[1,1024,7168]{2,1,0:T(8,128)(2,1)}) %all-gather.3.cloned.1.call-update) | async-done | bytes 14680080 | tf_op jit(solution)/shard_map/all_gather | solution.py:35
  261.5 65.9 %multiply_convert_fusion = bf16[3584,7168]{1,0:T(8,128)(2,1)} fusion(bf16[1024,7168]{1,0:T(8,128)(2,1)} %bitcast.47, f32[7168]{0:T(1024)S(1)} %add_rsqrt_fusion, f32[7168]{0:T(1024)S(1)} %broadcast_multiply_fusion, bf16[1024,3584]{1,0:T(8,128)(2,1)} %constant_dynamic-update-slice_fusion, f32[3584]{0:T(1024)S(1)} %add_rsqrt_fusion.1, ...), kind=kOutput, calls=%fused_computation.5 | convolution fusion | flops 52708769792 | bytes 73486336 | tf_op jit(solution)/shard_map/dot_general | solution.py:71
  327.4 0.0 reduce-scatter.5.cloned.1.call-update
  327.5 0.0 copy-start.1
  327.5 13.1 %gather_fusion.2 = bf16[1792,1024]{1,0:T(8,128)(2,1)} fusion(bf16[3584,1024]{1,0:T(8,128)(2,1)} %param.9, s32[2048]{0:T(1024)S(1)} %pad_clamp_fusion.1), kind=kCustom, calls=%fused_computation.2 | custom fusion | bytes 7347200 | tf_op jit(solution)/shard_map/gather | solution.py:52
  340.6 2.4 collective-permute-start.1
  343.0 2.6 collective-permute-start.2
  345.6 0.1 compare_select_fusion.4
  345.7 0.3 reduce-window.76
  346.0 0.3 reduce-window.74
  346.3 0.3 reduce-window.72
  346.6 0.1 slice.72
  346.6 0.1 reduce-window.73
  346.7 0.1 slice.74
  346.8 0.1 reduce-window.75
  346.8 0.1 slice.76
  346.9 0.1 reduce-window.77
  346.9 0.1 slice_reduce_fusion.2
  347.1 0.1 slice_reduce_fusion
  347.2 0.1 compare_select_fusion
  347.4 233.0 %collective-permute-done.1 = bf16[1792,1024]{1,0:T(8,128)(2,1)} collective-permute-done((bf16[1792,1024]{1,0:T(8,128)(2,1)}, bf16[1792,1024]{1,0:T(8,128)(2,1)}, u32[]{:S(2)}, u32[]{:S(2)}) %collective-permute-start.1) | collective-permute-done | bytes 3670048 | tf_op jit(solution)/shard_map/ppermute | solution.py:58
  580.4 78.8 %collective-permute-done.2 = bf16[1792,1024]{1,0:T(8,128)(2,1)} collective-permute-done((bf16[1792,1024]{1,0:T(8,128)(2,1)}, bf16[1792,1024]{1,0:T(8,128)(2,1)}, u32[]{:S(2)}, u32[]{:S(2)}) %collective-permute-start.2) | collective-permute-done | bytes 3670048 | tf_op jit(solution)/shard_map/ppermute | solution.py:66
  659.2 23.0 %pad_maximum_fusion = bf16[8960,1024]{1,0:T(8,128)(2,1)} fusion(bf16[1792,1024]{1,0:T(8,128)(2,1)} %collective-permute-done.3, bf16[1792,1024]{1,0:T(8,128)(2,1)} %collective-permute-done.2, bf16[1792,1024]{1,0:T(8,128)(2,1)} %collective-permute-done.1, bf16[3584,1024]{1,0:T(8,128)(2,1)} %param.9), kind=kLoop, calls=%fused_computation.13 | loop fusion | flops 73400320 | bytes 36700160 | tf_op jit(solution)/shard_map/concatenate | solution.py:103
  682.2 25.0 %gather_fusion.3 = bf16[3584,1024]{1,0:T(8,128)(2,1)} fusion(bf16[8960,1024]{1,0:T(8,128)(2,1)} %pad_maximum_fusion, s32[4096]{0:T(1024)S(1)} %pad_clamp_fusion), kind=kCustom, calls=%fused_computation.3 | custom fusion | bytes 14694400 | tf_op jit(solution)/shard_map/gather | solution.py:104
  707.2 23.6 %gather_fusion.4 = bf16[1792]{0:T(1024)(128)(2,1)S(1)} fusion(bf16[1792,7168]{1,0:T(8,128)(2,1)} %reduce-scatter.5.cloned.1.call-done, s32[1792]{0:T(1024)S(1)} %fusion.17), kind=kCustom, calls=%fused_computation.4 | custom fusion | bytes 21504 | tf_op jit(solution)/shard_map/jit(take_along_axis)/gather | solution.py:81
  730.8 0.2 select_dynamic-update-slice_fusion
  731.0 12.4 %psum.39 = f32[3584]{0:T(1024)S(1)} all-reduce(f32[3584]{0:T(1024)S(1)} %select_dynamic-update-slice_fusion), channel_id=1, replica_groups=mesh['layer'=2,'row'=4,'col'=2,'sub'=2] {'col','sub'}, use_global_device_ids=true, to_apply=%region_15.16 | all-reduce | flops 3584 | bytes 28672 | tf_op jit(solution)/shard_map/psum | solution.py:88
  743.3 9.5 %divide_convert_fusion = bf16[3584,1024]{1,0:T(8,128)(2,1)} fusion(bf16[3584,1024]{1,0:T(8,128)(2,1)} %gather_fusion.3, bf16[3584,1024]{1,0:T(8,128)(2,1)} %param.8, f32[3584]{0:T(1024)S(1)} %get-tuple-element.37, f32[3584]{0:T(1024)S(1)} %get-tuple-element.36), kind=kLoop, calls=%fused_computation.14 | loop fusion | flops 22020096 | bytes 22048768 | tf_op jit(solution)/shard_map/convert_element_type | solution.py:106
  (23 shorter events, 0.2 us)
Async XLA Ops:
  7.2 254.3 %all-gather.3.cloned.1.call-start = ((), (), s32[]{:S(2)}) async-start(), calls=%async_computation.1 | async-start | bytes 18350080 | tf_op jit(solution)/shard_map/all_gather | solution.py:35
  7.9 699.3 %reduce-scatter.5.cloned.1.call-start = ((), (), s32[]{:S(2)}) async-start(), calls=%async_computation.2 | async-start | bytes 77070336
  7.9 185.5 %collective-permute-start = (bf16[512,3584]{1,0:T(8,128)(2,1)}, bf16[512,3584]{1,0:T(8,128)(2,1)}, u32[]{:S(2)}, u32[]{:S(2)}) collective-permute-start(bf16[512,3584]{1,0:T(8,128)(2,1)} %bitcast.46), channel_id=1, source_target_pairs={{0,2},{2,0},{1,3},{3,1},{4,6},{6,4},{5,7},{7,5},{8,10},{10,8},{9,1... | collective-permute-start | bytes 11010056 | tf_op jit(solution)/shard_map/ppermute | solution.py:39
  187.7 3.7 copy-start
  327.5 18.1 %copy-start.1 = (s32[14336]{0:T(1024)S(1)}, s32[14336]{0:T(1024)}, u32[]{:S(2)}) copy-start(s32[14336]{0:T(1024)} %param.7) | copy-start | bytes 172036
  340.6 239.7 %collective-permute-start.1 = (bf16[1792,1024]{1,0:T(8,128)(2,1)}, bf16[1792,1024]{1,0:T(8,128)(2,1)}, u32[]{:S(2)}, u32[]{:S(2)}) collective-permute-start(bf16[1792,1024]{1,0:T(8,128)(2,1)} %gather_fusion.2), channel_id=1, source_target_pairs={{0,8},{4,12},{8,0},{12,4},{1,9},{5,13},{9,1},{13,5},{2,10},{6,14},... | collective-permute-start | bytes 11010056 | tf_op jit(solution)/shard_map/ppermute | solution.py:58
  343.0 316.2 %collective-permute-start.2 = (bf16[1792,1024]{1,0:T(8,128)(2,1)}, bf16[1792,1024]{1,0:T(8,128)(2,1)}, u32[]{:S(2)}, u32[]{:S(2)}) collective-permute-start(bf16[1792,1024]{1,0:T(8,128)(2,1)} %gather_fusion), channel_id=1, source_target_pairs={{0,12},{4,8},{8,4},{12,0},{1,13},{5,9},{9,5},{13,1},{2,14},{6,10},... | collective-permute-start | bytes 11010056 | tf_op jit(solution)/shard_map/ppermute | solution.py:66
  345.6 313.6 %collective-permute-start.3 = (bf16[1792,1024]{1,0:T(8,128)(2,1)}, bf16[1792,1024]{1,0:T(8,128)(2,1)}, u32[]{:S(2)}, u32[]{:S(2)}) collective-permute-start(bf16[1792,1024]{1,0:T(8,128)(2,1)} %gather_fusion.1), channel_id=1, source_target_pairs={{0,4},{4,0},{8,12},{12,8},{1,5},{5,1},{9,13},{13,9},{2,6},{6,2},{1... | collective-permute-start | bytes 11010056 | tf_op jit(solution)/shard_map/ppermute | solution.py:66
Sparse Core Ops, SparseCore 0:
  9.6 251.8 all-gather.2
  327.6 65.9 reduce-scatter.4
